TPU v7x, 32 devices: a whole 2x2x4 slice. The times are simulated.
32 devices in a mesh: wide: 8 (over z, x), narrow: 4 (over y, core).
Axes of the slice: x: 2, y: 2, z: 4, core: 2. Of those that a mesh axis runs over, the one named last changes fastest.
Arguments:
- treated: bfloat16 [8192, 512], P(('wide', 'narrow')), may hold values from -6 to 6
- control: bfloat16 [8192, 512], P('wide'), may hold values from -6 to 6
- treated_weight: float32 [8192], P(('wide', 'narrow')), may hold values from 0.5 to 2
- control_weight: float32 [8192], replicated, may hold values from 0.5 to 2
- band: int32 [64, 24], P(('wide', 'narrow')), may hold values from 0 to 1, as said below
Outputs:
- grad_treated: float32 [8192, 512], P(('wide', 'narrow'))
- grad_control: float32 [8192, 512], P(('wide', 'narrow'))
Inputs may be any that keep to these rules, and one draw needn't show every extreme that they name: band[t, k] = 1 pairs treated block t with control block (t // 8 - 1) * 8 + k. For each t the ones form one run of k that contains k = 8 + t % 8; every k whose control block lies outside 0 to 63 is 0.
All inputs are finite; a program needn't handle non-finite values.
Results may differ from a plain program's by a relative error of at most 0.0055.
Values may be sent and summed in bfloat16 or wider, within the bound.
A program may use at most 64 MiB of HBM per device.

v0:
```python
import jax
import jax.numpy as jnp
from jax import lax
from jax.sharding import PartitionSpec as P

SWEEPS = 2


SMOOTHING_TEMP = 0.05
EPSILON = 1e-06


def extended(block, sides, width):
    for axis, dim in sides:
        count = lax.axis_size(axis)
        forward = [(i, i + 1) for i in range(count - 1)]
        backward = [(target, source) for source, target in forward]
        low = lax.ppermute(
            lax.slice_in_dim(block, block.shape[dim] - width, None, axis=dim), axis, forward
        )
        high = lax.ppermute(lax.slice_in_dim(block, 0, width, axis=dim), axis, backward)
        block = jnp.concatenate([low, block, high], axis=dim)
    return block


def normalize(features):
    values = features.astype(jnp.float32)
    return (values * lax.rsqrt(jnp.mean(values * values, axis=1, keepdims=True) + EPSILON)).astype(
        jnp.bfloat16
    )


def expand(pair_blocks, block_rows):
    block_count, column_count = pair_blocks.shape
    full = jnp.broadcast_to(
        pair_blocks[:, None, :, None], (block_count, block_rows, column_count, block_rows)
    )
    return full.reshape(block_count * block_rows, column_count * block_rows)


def shards(treated, control, treated_weight, control_weight, band):
    row_count = treated.shape[0]
    slab_rows = control.shape[0]
    feature_total = treated.shape[1]
    block_rows = row_count // band.shape[0]
    wide_index = lax.axis_index("wide")
    narrow_index = lax.axis_index("narrow")
    treated_norm = normalize(treated)
    own_slab = normalize(control)
    band_span = extended(own_slab[None], (("wide", 0),), 1)
    band_span = band_span.reshape(3 * slab_rows, feature_total)
    paired_mask = expand(band, block_rows) > 0
    scale_factor = 1.0 / (feature_total * SMOOTHING_TEMP)
    pairwise_inner = lax.dot_general(
        treated_norm, band_span, (((1,), (1,)), ((), ())), preferred_element_type=jnp.float32
    )
    kernel = jnp.where(paired_mask, jnp.exp(pairwise_inner * scale_factor), 0.0)
    scales = jnp.ones((3 * slab_rows,), jnp.float32)
    own_weight_slab = lax.dynamic_slice_in_dim(control_weight, wide_index * slab_rows, slab_rows)
    row_scale = treated_weight
    for sweep_index in range(SWEEPS):
        row_scale = treated_weight / jnp.sum(kernel * scales[None, :], axis=1)
        column_parts = jnp.sum(kernel * row_scale[:, None], axis=0).reshape(3, slab_rows)
        slab_parts = lax.psum(column_parts, "narrow")
        edges = extended(slab_parts[None], (("wide", 0),), 1)
        column_total = edges[1, 1] + edges[0, 2] + edges[2, 0]
        col_scale = own_weight_slab / column_total
        scales = extended(col_scale[None], (("wide", 0),), 1).reshape(3 * slab_rows)
    transport = row_scale[:, None] * kernel * scales[None, :]
    plan_bf = transport.astype(jnp.bfloat16)
    pulled = jnp.dot(plan_bf, band_span, preferred_element_type=jnp.float32)
    grad_treated = jnp.sum(transport, axis=1)[:, None] * treated_norm.astype(jnp.float32) - pulled
    quarter = slab_rows // lax.axis_size("narrow")
    pushed = lax.dot_general(
        plan_bf, treated_norm, (((0,), (0,)), ((), ())), preferred_element_type=jnp.float32
    )
    pushed = pushed.reshape(3, slab_rows, feature_total)
    neighbours = extended(pushed, (("wide", 0),), 1)
    summed = lax.psum_scatter(
        neighbours[0] + neighbours[2] + neighbours[4], "narrow", scatter_dimension=0, tiled=True
    )
    own_rows = lax.dynamic_slice_in_dim(own_slab, narrow_index * quarter, quarter, 0).astype(
        jnp.float32
    )
    own_weight = lax.dynamic_slice_in_dim(
        control_weight, wide_index * slab_rows + narrow_index * quarter, quarter
    )
    grad_control = own_weight[:, None] * own_rows - summed
    return (grad_treated, grad_control)


def solution(mesh):
    return jax.shard_map(
        shards,
        mesh=mesh,
        in_specs=(
            P(("wide", "narrow"), None),
            P("wide", None),
            P(("wide", "narrow")),
            P(),
            P(("wide", "narrow"), None),
        ),
        out_specs=(P(("wide", "narrow"), None), P(("wide", "narrow"), None)),
        check_vma=False,
    )
```

profile of v0, /device:TPU:0, one launch (start us, length us, event | category | flops | bytes accessed | tf_op | source)
XLA Modules:
  0.0 259.0 jit_solution(17032125562029713475)
XLA Ops:
  7.2 0.0 reduce-scatter.2.cloned.1.call-start
  7.2 1.5 fusion.2
  8.8 1.5 fusion.13
  10.3 1.3 collective-permute-start.1
  11.6 5.5 %collective-permute-start = (bf16[1,1024,512]{2,1,0:T(8,128)(2,1)S(1)}, bf16[1,1024,512]{2,1,0:T(8,128)(2,1)S(1)}, u32[]{:S(2)}, u32[]{:S(2)}) collective-permute-start(bf16[1,1024,512]{2,1,0:T(8,128)(2,1)S(1)} %fusion.13), channel_id=1, source_target_pairs={{0,4},{4,8},{8,12},{12,16},{16,20},{20,24},{24,28},{1,5},{5,9},{9,... | collective-permute-start | bytes 3145736 | tf_op jit(solution)/shard_map/ppermute | solution.py:18
  17.1 0.1 fusion.5
  17.3 21.0 %collective-permute-done.1 = bf16[1,1024,512]{2,1,0:T(8,128)(2,1)S(1)} collective-permute-done((bf16[1,1024,512]{2,1,0:T(8,128)(2,1)S(1)}, bf16[1,1024,512]{2,1,0:T(8,128)(2,1)S(1)}, u32[]{:S(2)}, u32[]{:S(2)}) %collective-permute-start.1) | collective-permute-done | bytes 1048608 | tf_op jit(solution)/shard_map/ppermute | solution.py:21
  38.3 22.6 %collective-permute-done = bf16[1,1024,512]{2,1,0:T(8,128)(2,1)S(1)} collective-permute-done((bf16[1,1024,512]{2,1,0:T(8,128)(2,1)S(1)}, bf16[1,1024,512]{2,1,0:T(8,128)(2,1)S(1)}, u32[]{:S(2)}, u32[]{:S(2)}) %collective-permute-start) | collective-permute-done | bytes 1048608 | tf_op jit(solution)/shard_map/ppermute | solution.py:18
  60.9 0.3 pad_maximum_fusion
  61.3 0.3 broadcast_in_dim.16
  61.5 0.0 copy-start.3
  61.6 1.3 fusion.10
  62.8 0.1 copy-done
  62.9 0.4 multiply_reduce_fusion.1
  63.3 11.2 %psum.14 = f32[1,3,1024]{2,1,0:T(4,128)S(1)} all-reduce(f32[1,3,1024]{2,1,0:T(4,128)S(1)} %broadcast_in_dim.35), channel_id=1, replica_groups=mesh['wide'=8,'narrow'=4] {'narrow'}, use_global_device_ids=true, to_apply=%region_4.5 | all-reduce | flops 3072 | bytes 24576 | tf_op jit(solution)/shard_map/psum | solution.py:64
  74.6 1.3 collective-permute-start.3
  75.8 5.0 %collective-permute-start.2 = (f32[1,3,1024]{2,1,0:T(4,128)S(1)}, f32[1,3,1024]{2,1,0:T(4,128)S(1)}, u32[]{:S(2)}, u32[]{:S(2)}) collective-permute-start(f32[1,3,1024]{2,1,0:T(4,128)S(1)} %psum.14), channel_id=1, source_target_pairs={{0,4},{4,8},{8,12},{12,16},{16,20},{20,24},{24,28},{1,5},{5,9},{9,... | collective-permute-start | bytes 36872 | tf_op jit(solution)/shard_map/ppermute | solution.py:18
  80.9 0.0 collective-permute-done.3
  80.9 1.4 collective-permute-done.2
  82.3 0.7 dynamic-slice_divide_fusion.1
  83.0 1.3 collective-permute-start.5
  84.3 5.4 %collective-permute-start.4 = (f32[1,1024]{1,0:T(1,128)S(1)}, f32[1,1024]{1,0:T(1,128)S(1)}, u32[]{:S(2)}, u32[]{:S(2)}) collective-permute-start(f32[1,1024]{1,0:T(1,128)S(1)} %bitcast.28), channel_id=1, source_target_pairs={{0,4},{4,8},{8,12},{12,16},{16,20},{20,24},{24,28},{1,5},{5,9},{9,... | collective-permute-start | bytes 12296 | tf_op jit(solution)/shard_map/ppermute | solution.py:18
  89.8 0.0 collective-permute-done.5
  89.8 1.3 collective-permute-done.4
  91.1 0.3 multiply_reduce_fusion
  91.4 0.4 multiply_reduce_fusion.3
  91.8 10.2 %psum.15 = f32[1,3,1024]{2,1,0:T(4,128)S(1)} all-reduce(f32[1,3,1024]{2,1,0:T(4,128)S(1)} %broadcast_in_dim.37), channel_id=1, replica_groups=mesh['wide'=8,'narrow'=4] {'narrow'}, use_global_device_ids=true, to_apply=%region_7.8 | all-reduce | flops 3072 | bytes 24576 | tf_op jit(solution)/shard_map/psum | solution.py:64
  102.0 1.3 collective-permute-start.7
  103.3 5.7 %collective-permute-start.6 = (f32[1,3,1024]{2,1,0:T(4,128)S(1)}, f32[1,3,1024]{2,1,0:T(4,128)S(1)}, u32[]{:S(2)}, u32[]{:S(2)}) collective-permute-start(f32[1,3,1024]{2,1,0:T(4,128)S(1)} %psum.15), channel_id=1, source_target_pairs={{0,4},{4,8},{8,12},{12,16},{16,20},{20,24},{24,28},{1,5},{5,9},{9,... | collective-permute-start | bytes 36872 | tf_op jit(solution)/shard_map/ppermute | solution.py:18
  109.1 1.4 collective-permute-done.6
  110.5 0.7 dynamic-slice_divide_fusion
  111.2 1.3 collective-permute-start.9
  112.5 5.7 %collective-permute-start.8 = (f32[1,1024]{1,0:T(1,128)S(1)}, f32[1,1024]{1,0:T(1,128)S(1)}, u32[]{:S(2)}, u32[]{:S(2)}) collective-permute-start(f32[1,1024]{1,0:T(1,128)S(1)} %bitcast.25), channel_id=1, source_target_pairs={{0,4},{4,8},{8,12},{12,16},{16,20},{20,24},{24,28},{1,5},{5,9},{9,... | collective-permute-start | bytes 12296 | tf_op jit(solution)/shard_map/ppermute | solution.py:18
  118.2 1.3 collective-permute-done.8
  119.5 1.1 fusion.7
  120.7 0.4 slice_bitcast_fusion.1
  121.1 1.3 collective-permute-start.11
  122.4 5.9 %collective-permute-start.10 = (f32[1,1024,512]{2,1,0:T(8,128)S(1)}, f32[1,1024,512]{2,1,0:T(8,128)S(1)}, u32[]{:S(2)}, u32[]{:S(2)}) collective-permute-start(f32[1,1024,512]{2,1,0:T(8,128)S(1)} %get-tuple-element.2), channel_id=1, source_target_pairs={{0,4},{4,8},{8,12},{12,16},{16,20},{20,24},{24,28},{1,5},{5,9},{9,... | collective-permute-start | bytes 6291464 | tf_op jit(solution)/shard_map/ppermute | solution.py:18
  128.3 40.0 %collective-permute-done.11 = f32[1,1024,512]{2,1,0:T(8,128)S(1)} collective-permute-done((f32[1,1024,512]{2,1,0:T(8,128)S(1)}, f32[1,1024,512]{2,1,0:T(8,128)S(1)}, u32[]{:S(2)}, u32[]{:S(2)}) %collective-permute-start.11) | collective-permute-done | bytes 2097184 | tf_op jit(solution)/shard_map/ppermute | solution.py:21
  168.3 45.3 %collective-permute-done.10 = f32[1,1024,512]{2,1,0:T(8,128)S(1)} collective-permute-done((f32[1,1024,512]{2,1,0:T(8,128)S(1)}, f32[1,1024,512]{2,1,0:T(8,128)S(1)}, u32[]{:S(2)}, u32[]{:S(2)}) %collective-permute-start.10) | collective-permute-done | bytes 2097184 | tf_op jit(solution)/shard_map/ppermute | solution.py:18
  213.7 2.1 fusion.4
  215.8 0.0 reduce-scatter.2.cloned.1.call-update
  215.8 0.8 dynamic_slice.10
  216.6 2.7 %fusion.3 = bf16[1024,512]{1,0:T(8,128)(2,1)} fusion(bf16[1024,512]{1,0:T(8,128)(2,1)} %param.6, f32[1024]{0:T(1024)S(1)} %add_rsqrt_fusion), kind=kLoop, calls=%fused_computation.12 | loop fusion | flops 1572864 | bytes 2101248 | tf_op jit(solution)/shard_map/convert_element_type | solution.py:28
  219.3 0.5 multiply_reduce_fusion.2
  219.7 1.8 convolution_subtract_fusion
  221.6 28.5 %reduce-scatter.2.cloned.1.call-done = f32[256,512]{1,0:T(8,128)} async-done(((f32[1024,512]{1,0:T(8,128)}), f32[256,512]{1,0:T(8,128)}) %reduce-scatter.2.cloned.1.call-update) | async-done | bytes 524304 | tf_op jit(solution)/shard_map/reduce_scatter | solution.py:79
  250.1 2.0 multiply_subtract_fusion
  (23 shorter events, 0.2 us)
Async XLA Ops:
  7.2 10.0 %copy-start.2 = (bf16[256,512]{1,0:T(8,128)(2,1)S(1)}, bf16[256,512]{1,0:T(8,128)(2,1)}, u32[]{:S(2)}) copy-start(bf16[256,512]{1,0:T(8,128)(2,1)} %param.5) | copy-start | bytes 786436
  7.2 10.1 %copy-start.4 = (s32[2,24]{1,0:T(2,128)S(1)}, s32[2,24]{1,0:T(2,128)}, u32[]{:S(2)}) copy-start(s32[2,24]{1,0:T(2,128)} %param.9) | copy-start | bytes 580
  7.2 242.9 %reduce-scatter.2.cloned.1.call-start = ((), (), s32[]{:S(2)}) async-start(), calls=%async_computation.1 | async-start | bytes 2621440 | tf_op jit(solution)/shard_map/reduce_scatter | solution.py:79
  10.3 28.0 %collective-permute-start.1 = (bf16[1,1024,512]{2,1,0:T(8,128)(2,1)S(1)}, bf16[1,1024,512]{2,1,0:T(8,128)(2,1)S(1)}, u32[]{:S(2)}, u32[]{:S(2)}) collective-permute-start(bf16[1,1024,512]{2,1,0:T(8,128)(2,1)S(1)} %fusion.13), channel_id=1, source_target_pairs={{4,0},{8,4},{12,8},{16,12},{20,16},{24,20},{28,24},{5,1},{9,5},{13... | collective-permute-start | bytes 3145736 | tf_op jit(solution)/shard_map/ppermute | solution.py:21
  11.6 49.3 %collective-permute-start = (bf16[1,1024,512]{2,1,0:T(8,128)(2,1)S(1)}, bf16[1,1024,512]{2,1,0:T(8,128)(2,1)S(1)}, u32[]{:S(2)}, u32[]{:S(2)}) collective-permute-start(bf16[1,1024,512]{2,1,0:T(8,128)(2,1)S(1)} %fusion.13), channel_id=1, source_target_pairs={{0,4},{4,8},{8,12},{12,16},{16,20},{20,24},{24,28},{1,5},{5,9},{9,... | collective-permute-start | bytes 3145736 | tf_op jit(solution)/shard_map/ppermute | solution.py:18
  61.3 1.7 copy-start
  61.5 1.4 copy-start.3
  74.6 6.3 %collective-permute-start.3 = (f32[1,3,1024]{2,1,0:T(4,128)S(1)}, f32[1,3,1024]{2,1,0:T(4,128)S(1)}, u32[]{:S(2)}, u32[]{:S(2)}) collective-permute-start(f32[1,3,1024]{2,1,0:T(4,128)S(1)} %psum.14), channel_id=1, source_target_pairs={{4,0},{8,4},{12,8},{16,12},{20,16},{24,20},{28,24},{5,1},{9,5},{13... | collective-permute-start | bytes 36872 | tf_op jit(solution)/shard_map/ppermute | solution.py:21
  75.8 6.4 %collective-permute-start.2 = (f32[1,3,1024]{2,1,0:T(4,128)S(1)}, f32[1,3,1024]{2,1,0:T(4,128)S(1)}, u32[]{:S(2)}, u32[]{:S(2)}) collective-permute-start(f32[1,3,1024]{2,1,0:T(4,128)S(1)} %psum.14), channel_id=1, source_target_pairs={{0,4},{4,8},{8,12},{12,16},{16,20},{20,24},{24,28},{1,5},{5,9},{9,... | collective-permute-start | bytes 36872 | tf_op jit(solution)/shard_map/ppermute | solution.py:18
  83.0 6.7 %collective-permute-start.5 = (f32[1,1024]{1,0:T(1,128)S(1)}, f32[1,1024]{1,0:T(1,128)S(1)}, u32[]{:S(2)}, u32[]{:S(2)}) collective-permute-start(f32[1,1024]{1,0:T(1,128)S(1)} %bitcast.27), channel_id=1, source_target_pairs={{4,0},{8,4},{12,8},{16,12},{20,16},{24,20},{28,24},{5,1},{9,5},{13... | collective-permute-start | bytes 12296 | tf_op jit(solution)/shard_map/ppermute | solution.py:21
  84.3 6.8 %collective-permute-start.4 = (f32[1,1024]{1,0:T(1,128)S(1)}, f32[1,1024]{1,0:T(1,128)S(1)}, u32[]{:S(2)}, u32[]{:S(2)}) collective-permute-start(f32[1,1024]{1,0:T(1,128)S(1)} %bitcast.28), channel_id=1, source_target_pairs={{0,4},{4,8},{8,12},{12,16},{16,20},{20,24},{24,28},{1,5},{5,9},{9,... | collective-permute-start | bytes 12296 | tf_op jit(solution)/shard_map/ppermute | solution.py:18
  102.0 7.0 %collective-permute-start.7 = (f32[1,3,1024]{2,1,0:T(4,128)S(1)}, f32[1,3,1024]{2,1,0:T(4,128)S(1)}, u32[]{:S(2)}, u32[]{:S(2)}) collective-permute-start(f32[1,3,1024]{2,1,0:T(4,128)S(1)} %psum.15), channel_id=1, source_target_pairs={{4,0},{8,4},{12,8},{16,12},{20,16},{24,20},{28,24},{5,1},{9,5},{13... | collective-permute-start | bytes 36872 | tf_op jit(solution)/shard_map/ppermute | solution.py:21
  103.3 7.2 %collective-permute-start.6 = (f32[1,3,1024]{2,1,0:T(4,128)S(1)}, f32[1,3,1024]{2,1,0:T(4,128)S(1)}, u32[]{:S(2)}, u32[]{:S(2)}) collective-permute-start(f32[1,3,1024]{2,1,0:T(4,128)S(1)} %psum.15), channel_id=1, source_target_pairs={{0,4},{4,8},{8,12},{12,16},{16,20},{20,24},{24,28},{1,5},{5,9},{9,... | collective-permute-start | bytes 36872 | tf_op jit(solution)/shard_map/ppermute | solution.py:18
  111.2 7.0 %collective-permute-start.9 = (f32[1,1024]{1,0:T(1,128)S(1)}, f32[1,1024]{1,0:T(1,128)S(1)}, u32[]{:S(2)}, u32[]{:S(2)}) collective-permute-start(f32[1,1024]{1,0:T(1,128)S(1)} %bitcast.24), channel_id=1, source_target_pairs={{4,0},{8,4},{12,8},{16,12},{20,16},{24,20},{28,24},{5,1},{9,5},{13... | collective-permute-start | bytes 12296 | tf_op jit(solution)/shard_map/ppermute | solution.py:21
  112.5 7.0 %collective-permute-start.8 = (f32[1,1024]{1,0:T(1,128)S(1)}, f32[1,1024]{1,0:T(1,128)S(1)}, u32[]{:S(2)}, u32[]{:S(2)}) collective-permute-start(f32[1,1024]{1,0:T(1,128)S(1)} %bitcast.25), channel_id=1, source_target_pairs={{0,4},{4,8},{8,12},{12,16},{16,20},{20,24},{24,28},{1,5},{5,9},{9,... | collective-permute-start | bytes 12296 | tf_op jit(solution)/shard_map/ppermute | solution.py:18
  121.1 47.2 %collective-permute-start.11 = (f32[1,1024,512]{2,1,0:T(8,128)S(1)}, f32[1,1024,512]{2,1,0:T(8,128)S(1)}, u32[]{:S(2)}, u32[]{:S(2)}) collective-permute-start(f32[1,1024,512]{2,1,0:T(8,128)S(1)} %get-tuple-element.3), channel_id=1, source_target_pairs={{4,0},{8,4},{12,8},{16,12},{20,16},{24,20},{28,24},{5,1},{9,5},{13... | collective-permute-start | bytes 6291464 | tf_op jit(solution)/shard_map/ppermute | solution.py:21
  122.4 91.2 %collective-permute-start.10 = (f32[1,1024,512]{2,1,0:T(8,128)S(1)}, f32[1,1024,512]{2,1,0:T(8,128)S(1)}, u32[]{:S(2)}, u32[]{:S(2)}) collective-permute-start(f32[1,1024,512]{2,1,0:T(8,128)S(1)} %get-tuple-element.2), channel_id=1, source_target_pairs={{0,4},{4,8},{8,12},{12,16},{16,20},{20,24},{24,28},{1,5},{5,9},{9,... | collective-permute-start | bytes 6291464 | tf_op jit(solution)/shard_map/ppermute | solution.py:18
  216.6 3.1 %copy-start.1 = (bf16[3,1024,512]{2,1,0:T(8,128)(2,1)S(1)}, bf16[3,1024,512]{2,1,0:T(8,128)(2,1)}, u32[]{:S(2)}) copy-start(bf16[3,1024,512]{2,1,0:T(8,128)(2,1)} %copy-done) | copy-start | bytes 9437188
Sparse Core Ops, SparseCore 0:
  215.9 34.0 reduce-scatter.1
where the time goes:
time: 260 us; the launch traced here: 259 us
  waiting for transfers between devices  163 us (63%)
  starting transfers between devices  41 us (16%)
  blocking collectives  21.4 us (8%)
  between operations  14.3 us (6%)
  other arithmetic  13.4 us (5%)
  matrix products  4.23 us (2%)
    ppermute x6, waiting for transfers between devices, extended(): lax.ppermute(lax.slice_in_dim(block, block.shape[dim] - width, None, axis...  73.4 us
    ppermute x6, waiting for transfers between devices, extended(): lax.ppermute(lax.slice_in_dim(block, 0, width, axis=dim), axis, backward)  61 us
    ppermute x6, starting transfers between devices, extended(): lax.ppermute(lax.slice_in_dim(block, block.shape[dim] - width, None, axis...  33.3 us
    reduce_scatter x1, waiting for transfers between devices, shards(): lax.psum_scatter(neighbours[0] + neighbours[2] + neighbours[4], 'narrow',...  28.5 us
    psum x2, blocking collectives, shards(): slab_parts = lax.psum(column_parts, 'narrow')  21.4 us
    ppermute x6, starting transfers between devices, extended(): lax.ppermute(lax.slice_in_dim(block, 0, width, axis=dim), axis, backward)  7.71 us
  transfers between devices with their start and end apart: 13, of which 9 were waited for; matrix products, arithmetic and copies ran while one was open for 2% of the time, Pallas kernels for 0%

commit v1 on v0

v1 whole, which is shorter than its diff:
```python
import functools

import jax
import jax.numpy as jnp
from jax import lax
from jax.experimental import pallas as pl
from jax.experimental.pallas import tpu as pltpu
from jax.sharding import PartitionSpec as P

SWEEPS = 2
SMOOTHING_TEMP = 0.05
EPSILON = 1e-06
LANES = 128
CHUNKS = 4
OWN, NEAR, FAR = 0, 1, 2
MESH = pl.DeviceIdType.MESH
F32 = jnp.float32
BF16 = jnp.bfloat16


def normalize(block):
    values = block.astype(F32)
    return (
        values * lax.rsqrt(jnp.mean(values * values, axis=1, keepdims=True) + EPSILON)
    ).astype(BF16)


def to_columns(row):
    return jnp.transpose(jnp.broadcast_to(row, (LANES, row.shape[1])))


def lane_sums(parts):
    return jnp.sum(jnp.transpose(parts), axis=0, keepdims=True)


def body(
    wide_size, narrow_size, scale,
    t_ref, c_ref, tw_ref, cw_ref, band_ref, gt_ref, gc_ref,
    tn, cn, kmat, plan, aux, aux_in, rs, rr, cs, cr,
    far_out, far_in, near_sum, near_out, near_in, own_pull,
    pair_out, pair_in, cross_out, cross_in,
    bulk_sem, relay_sem, aux_sem, row_sem, col_sem, far_sem, near_sem, pair_sem, cross_sem,
):
    w = lax.axis_index("wide")
    n = lax.axis_index("narrow")
    rows, features = t_ref.shape
    slab = c_ref.shape[0]
    blocks = slab // LANES
    block_rows = rows // band_ref.shape[0]
    step = 1 - 2 * (w % 2)
    near, far = w + step, w - step
    near2, far2 = w + 2 * step, w - 2 * step
    has_far = (far >= 0) & (far < wide_size)
    has_near2 = (near2 >= 0) & (near2 < wide_size)
    pair = n + 1 - 2 * (n % 2)
    cross = (n + 2) % narrow_size
    cross_pair = (pair + 2) % narrow_size

    def copy(src, dst, sems, index, wide, narrow):
        return pltpu.make_async_remote_copy(
            src_ref=src, dst_ref=dst,
            send_sem=sems.at[(0,) + index], recv_sem=sems.at[(1,) + index],
            device_id=(wide, narrow), device_id_type=MESH,
        )

    barrier = pltpu.get_barrier_semaphore()

    def greet(wide, narrow):
        pl.semaphore_signal(barrier, inc=1, device_id=(wide, narrow), device_id_type=MESH)

    greet(near, n)
    for other in range(1, narrow_size):
        greet(w, (n + other) % narrow_size)

    @pl.when(has_far)
    def _():
        greet(far, n)
        greet(far2, n)

    @pl.when(has_near2)
    def _():
        greet(near2, n)

    tn[OWN] = normalize(t_ref[...])
    for side in range(3):
        for block in range(blocks):
            k = side * blocks + block
            aux[side, 0:2, block * LANES:(block + 1) * LANES] = jnp.broadcast_to(
                band_ref[:, k:k + 1].astype(F32), (2, LANES)
            )
        aux[side, 2:3, 0:rows] = tw_ref[...]

    @pl.when(jnp.logical_not(has_far))
    def _():
        tn[FAR] = jnp.zeros((rows, features), BF16)
        aux_in[1] = jnp.zeros(aux_in.shape[1:], F32)
        for sweep in range(SWEEPS):
            rr[sweep, 2] = jnp.ones((1, rows), F32)
            rr[sweep, 3] = jnp.zeros((1, rows), F32)
            rr[sweep, 5] = jnp.zeros((1, rows), F32)

    @pl.when(jnp.logical_not(has_near2))
    def _():
        far_in[...] = jnp.zeros((rows, features), BF16)
        for sweep in range(SWEEPS):
            rr[sweep, 4] = jnp.zeros((1, rows), F32)

    pl.semaphore_wait(barrier, narrow_size + has_far.astype(jnp.int32) * 2 + has_near2.astype(jnp.int32))

    size = rows // CHUNKS
    part = [pl.ds(chunk * size, size) for chunk in range(CHUNKS)]
    aux_near = copy(aux.at[step + 1], aux_in.at[0], aux_sem, (0,), near, n)
    aux_far = copy(aux.at[1 - step], aux_in.at[1], aux_sem, (1,), far, n)
    bulk = [
        copy(tn.at[OWN, part[i]], tn.at[NEAR, part[i]], bulk_sem, (i,), near, n)
        for i in range(CHUNKS)
    ]
    relay = [
        copy(tn.at[NEAR, part[i]], tn.at[FAR, part[i]], relay_sem, (i,), near2, n)
        for i in range(CHUNKS)
    ]
    aux_near.start()

    @pl.when(has_far)
    def _():
        aux_far.start()

    for item in bulk:
        item.start()

    for quarter in range(narrow_size):
        at = pl.ds(quarter * (slab // narrow_size), slab // narrow_size)
        cn[at, :] = normalize(c_ref[at, :])

    def kernel_block(shard, mask_ref):
        sums = []
        for block in range(rows // block_rows):
            at = slice(block * block_rows, (block + 1) * block_rows)
            inner = lax.dot_general(
                tn[shard, at, :], cn[...], (((1,), (1,)), ((), ())), preferred_element_type=F32
            )
            entries = jnp.where(mask_ref[block:block + 1, :] > 0, jnp.exp(inner * scale), 0.0)
            kmat[shard, at, :] = entries
            total = entries[:, 0:LANES]
            for j in range(1, blocks):
                total = total + entries[:, j * LANES:(j + 1) * LANES]
            sums.append(total)
        return jnp.concatenate(sums, axis=0)

    slot_of = {NEAR: 0, OWN: 1, FAR: 2}
    rs[0, slot_of[OWN]] = lane_sums(kernel_block(OWN, aux.at[1]))

    for i in range(CHUNKS):
        bulk[i].wait_recv()

        @pl.when(has_near2)
        def _(i=i):
            relay[i].start()

    aux_near.wait_recv()
    rs[0, slot_of[NEAR]] = lane_sums(kernel_block(NEAR, aux_in.at[0]))

    @pl.when(has_far)
    def _():
        aux_far.wait_recv()
        for i in range(CHUNKS):
            relay[i].wait_recv()

    rs[0, slot_of[FAR]] = lane_sums(kernel_block(FAR, aux_in.at[1]))

    weights = {
        OWN: tw_ref[...],
        NEAR: aux_in[0, 2:3, 0:rows],
        FAR: aux_in[1, 2:3, 0:rows],
    }
    cols = [slice(j * LANES, (j + 1) * LANES) for j in range(blocks)]
    own_mass = cw_ref[pl.ds(w, 1), :]
    col_scale = None
    row_scale = None
    for sweep in range(SWEEPS):
        if sweep:
            for shard in (OWN, NEAR, FAR):
                total = kmat[shard, :, cols[0]] * col_scale[:, cols[0]]
                for j in range(1, blocks):
                    total = total + kmat[shard, :, cols[j]] * col_scale[:, cols[j]]
                rs[sweep, slot_of[shard]] = lane_sums(total)
        to_near = copy(rs.at[sweep, pl.ds(0, 2)], rr.at[sweep, pl.ds(0, 2)], row_sem, (sweep, 0), near, n)
        to_far = copy(rs.at[sweep, pl.ds(1, 2)], rr.at[sweep, pl.ds(2, 2)], row_sem, (sweep, 1), far, n)
        to_near2 = copy(rs.at[sweep, pl.ds(0, 1)], rr.at[sweep, pl.ds(5, 1)], row_sem, (sweep, 2), near2, n)
        to_far2 = copy(rs.at[sweep, pl.ds(2, 1)], rr.at[sweep, pl.ds(4, 1)], row_sem, (sweep, 3), far2, n)

        @pl.when(has_far)
        def _(to_far=to_far, to_far2=to_far2):
            to_far.start()
            to_far2.start()

        @pl.when(has_near2)
        def _(to_near2=to_near2):
            to_near2.start()

        to_near.start()
        to_near.wait_recv()

        @pl.when(has_far)
        def _(to_far=to_far, to_near2=to_near2):
            to_far.wait_recv()
            to_near2.wait_recv()

        @pl.when(has_near2)
        def _(to_far2=to_far2):
            to_far2.wait_recv()

        totals = {
            OWN: rs[sweep, 1] + rr[sweep, 0] + rr[sweep, 3],
            NEAR: rs[sweep, 0] + rr[sweep, 1] + rr[sweep, 4],
            FAR: rs[sweep, 2] + rr[sweep, 2] + rr[sweep, 5],
        }
        row_scale = {shard: to_columns(weights[shard] / totals[shard]) for shard in totals}
        for j in range(blocks):
            total = jnp.zeros((8, LANES), F32)
            for shard in (OWN, NEAR, FAR):
                total = total + jnp.sum(
                    (kmat[shard, :, cols[j]] * row_scale[shard]).reshape(rows // 8, 8, LANES), axis=0
                )
            cs[sweep, :, cols[j]] = jnp.sum(total, axis=0, keepdims=True)
        sends = [
            copy(cs.at[sweep], cr.at[sweep, other - 1], col_sem, (sweep, other - 1), w, (n + other) % narrow_size)
            for other in range(1, narrow_size)
        ]
        for item in sends:
            item.start()
        for item in sends:
            item.wait_recv()
        total = cs[sweep]
        for other in range(narrow_size - 1):
            total = total + cr[sweep, other]
        col_scale = own_mass / total

    def plan_block(shard):
        total = jnp.zeros((rows, LANES), F32)
        for j in range(blocks):
            value = kmat[shard, :, cols[j]] * row_scale[shard] * col_scale[:, cols[j]]
            total = total + value
            plan[shard, :, cols[j]] = value.astype(BF16)
        return jnp.sum(total, axis=1, keepdims=True)

    def pull(shard, mass):
        pulled = jnp.dot(plan[shard], cn[...], preferred_element_type=F32)
        return mass * tn[shard].astype(F32) - pulled

    far_out[...] = pull(FAR, plan_block(FAR)).astype(BF16)
    far_send = [
        copy(far_out.at[part[i]], far_in.at[part[i]], far_sem, (i,), far2, n) for i in range(CHUNKS)
    ]

    @pl.when(has_far)
    def _():
        for item in far_send:
            item.start()

    near_mass = plan_block(NEAR)
    own_mass_rows = plan_block(OWN)

    quarter_rows = slab // narrow_size

    def push(quarter):
        at = pl.ds(pl.multiple_of(quarter * quarter_rows, quarter_rows), quarter_rows)
        total = jnp.zeros((quarter_rows, features), F32)
        for shard in (OWN, NEAR, FAR):
            total = total + lax.dot_general(
                plan[shard, :, at], tn[shard], (((0,), (0,)), ((), ())), preferred_element_type=F32
            )
        return total

    pair_send = [copy(pair_out.at[i], pair_in.at[i], pair_sem, (i,), w, pair) for i in range(2)]
    pair_out[0] = push(cross_pair).astype(BF16)
    pair_send[0].start()
    near_sum[...] = pull(NEAR, near_mass)
    own_push = push(cross)
    pair_send[0].wait_recv()
    cross_out[...] = (own_push + pair_in[0].astype(F32)).astype(BF16)
    cross_send = copy(cross_out, cross_in, cross_sem, (0,), w, cross)
    cross_send.start()
    pair_out[1] = push(pair).astype(BF16)
    pair_send[1].start()

    near_send = [
        copy(near_out.at[part[i]], near_in.at[part[i]], near_sem, (i,), near, n) for i in range(CHUNKS)
    ]
    for i in range(CHUNKS):
        @pl.when(has_near2)
        def _(i=i):
            far_send[i].wait_recv()

        near_out[part[i], :] = (near_sum[part[i], :] + far_in[part[i], :].astype(F32)).astype(BF16)
        near_send[i].start()

    own_pull[...] = pull(OWN, own_mass_rows)
    at = pl.ds(pl.multiple_of(n * quarter_rows, quarter_rows), quarter_rows)
    mass = to_columns(cw_ref[pl.ds(w, 1), at])
    own_rows = cn[at, :].astype(F32)
    own_push = push(n)
    pair_send[1].wait_recv()
    own_push = own_push + pair_in[1].astype(F32)
    for j in range(features // LANES):
        lanes = slice(j * LANES, (j + 1) * LANES)
        gc_ref[:, lanes] = mass * own_rows[:, lanes] - own_push[:, lanes]
    cross_send.wait_recv()
    gc_ref[...] = gc_ref[...] - cross_in[...].astype(F32)
    for i in range(CHUNKS):
        near_send[i].wait_recv()
        gt_ref[part[i], :] = own_pull[part[i], :] + near_in[part[i], :].astype(F32)

    aux_near.wait_send()
    for item in bulk + near_send + pair_send + [cross_send]:
        item.wait_send()
    for sweep in range(SWEEPS):
        copy(rs.at[sweep, pl.ds(0, 2)], rr.at[sweep, pl.ds(0, 2)], row_sem, (sweep, 0), near, n).wait_send()
        for other in range(1, narrow_size):
            copy(
                cs.at[sweep], cr.at[sweep, other - 1], col_sem, (sweep, other - 1), w, (n + other) % narrow_size
            ).wait_send()

    @pl.when(has_far)
    def _():
        aux_far.wait_send()
        for item in far_send:
            item.wait_send()
        for sweep in range(SWEEPS):
            copy(rs.at[sweep, pl.ds(1, 2)], rr.at[sweep, pl.ds(2, 2)], row_sem, (sweep, 1), far, n).wait_send()
            copy(rs.at[sweep, pl.ds(2, 1)], rr.at[sweep, pl.ds(4, 1)], row_sem, (sweep, 3), far2, n).wait_send()

    @pl.when(has_near2)
    def _():
        for item in relay:
            item.wait_send()
        for sweep in range(SWEEPS):
            copy(rs.at[sweep, pl.ds(0, 1)], rr.at[sweep, pl.ds(5, 1)], row_sem, (sweep, 2), near2, n).wait_send()


def shards(wide_size, narrow_size, treated, control, treated_weight, control_weight, band):
    rows, features = treated.shape
    slab = control.shape[0]
    quarter = slab // narrow_size
    vmem = pl.BlockSpec(memory_space=pltpu.VMEM)
    dma = lambda *shape: pltpu.SemaphoreType.DMA((2,) + shape)
    block = pltpu.VMEM((rows, features), BF16)
    scratch = [
        pltpu.VMEM((3, rows, features), BF16),
        pltpu.VMEM((slab, features), BF16),
        pltpu.VMEM((3, rows, slab), F32),
        pltpu.VMEM((3, rows, slab), BF16),
        pltpu.VMEM((3, 4, slab), F32),
        pltpu.VMEM((2, 4, slab), F32),
        pltpu.VMEM((SWEEPS, 3, 1, rows), F32),
        pltpu.VMEM((SWEEPS, 6, 1, rows), F32),
        pltpu.VMEM((SWEEPS, 1, slab), F32),
        pltpu.VMEM((SWEEPS, narrow_size - 1, 1, slab), F32),
        block, block,
        pltpu.VMEM((rows, features), F32),
        block, block,
        pltpu.VMEM((rows, features), F32),
        pltpu.VMEM((2, quarter, features), BF16),
        pltpu.VMEM((2, quarter, features), BF16),
        pltpu.VMEM((quarter, features), BF16),
        pltpu.VMEM((quarter, features), BF16),
        dma(CHUNKS), dma(CHUNKS), dma(2), dma(SWEEPS, 4), dma(SWEEPS, narrow_size - 1),
        dma(CHUNKS), dma(CHUNKS), dma(2), dma(1),
    ]
    scale = 1.0 / (features * SMOOTHING_TEMP)
    return pl.pallas_call(
        functools.partial(body, wide_size, narrow_size, scale),
        out_shape=(
            jax.ShapeDtypeStruct((rows, features), F32),
            jax.ShapeDtypeStruct((quarter, features), F32),
        ),
        in_specs=[vmem] * 5,
        out_specs=(vmem, vmem),
        scratch_shapes=scratch,
        compiler_params=pltpu.CompilerParams(
            collective_id=0, has_side_effects=True, vmem_limit_bytes=40 * 1024 * 1024
        ),
    )(
        treated,
        control,
        treated_weight.reshape(1, rows),
        control_weight.reshape(wide_size, slab),
        band,
    )


def solution(mesh):
    return jax.shard_map(
        functools.partial(shards, mesh.shape["wide"], mesh.shape["narrow"]),
        mesh=mesh,
        in_specs=(
            P(("wide", "narrow"), None),
            P("wide", None),
            P(("wide", "narrow")),
            P(),
            P(("wide", "narrow"), None),
        ),
        out_specs=(P(("wide", "narrow"), None), P(("wide", "narrow"), None)),
        check_vma=False,
    )
```

time: 260 us -> 45.7 us (0.18)
  waiting for transfers between devices: 163 us -> 0 us
  starting transfers between devices: 41 us -> 0 us
  Pallas kernels: 0 us -> 40.2 us
  blocking collectives: 21.4 us -> 0 us
  between operations: 14.3 us -> 0.68 us
  other arithmetic: 13.4 us -> 0 us
  matrix products: 4.23 us -> 0 us
  local copies, waits for them, and re-layouts: 1.62 us -> 4.55 us
    ppermute x12 -> x0, waiting for transfers between devices: 134 us -> none  [the longest x6 73.4 us: extended(): lax.ppermute(lax.slice_in_dim(block, block.shape[dim] - width, None, axis...]
    ppermute x12 -> x0, starting transfers between devices: 41 us -> none  [the longest x6 33.3 us: extended(): lax.ppermute(lax.slice_in_dim(block, block.shape[dim] - width, None, axis...]
    pallas_call x0 -> x1, Pallas kernels: none -> 40.2 us  [shards(): pl.pallas_call(functools.partial(body, wide_size, narrow_size, scale), ou...]
    reduce_scatter x1 -> x0, waiting for transfers between devices: 28.5 us -> none  [shards(): lax.psum_scatter(neighbours[0] + neighbours[2] + neighbours[4], 'narrow',...]
    psum x2 -> x0, blocking collectives: 21.4 us -> none  [shards(): slab_parts = lax.psum(column_parts, 'narrow')]
    dot_general x3 -> x0, matrix products: 4.23 us -> none  [the longest x1 1.81 us: shards(): pulled = jnp.dot(plan_bf, band_span, preferred_element_type=jnp.float32)]
    unnamed x10, local copies, waits for them, and re-layouts: 0.1 us -> 3.77 us
    reduce_sum x6 -> x0, other arithmetic: 3.2 us -> none  [the longest x2 1.66 us: normalize(): jnp.mean(values * values, axis=1, keepdims=True) + EPSILON]
  transfers between devices with their start and end apart: 13 -> 0, of which waited for: 9 -> 0; matrix products, arithmetic and copies ran while one was open for 2% -> 0% of each run, Pallas kernels for 0% -> 0%
where the time goes in v1:
time: 45.7 us; the launch traced here: 45.4 us
  Pallas kernels  40.2 us (88%)
  local copies, waits for them, and re-layouts  4.55 us (10%)
  between operations  0.68 us (1%)
    pallas_call x1, Pallas kernels, shards(): pl.pallas_call(functools.partial(body, wide_size, narrow_size, scale), ou...  40.2 us
    unnamed x10, local copies, waits for them, and re-layouts  3.77 us

profile of v1, /device:TPU:0, one launch (start us, length us, event | category | flops | bytes accessed | tf_op | source)
XLA Modules:
  0.0 45.4 jit_solution(3882908418740659440)
XLA Ops:
  0.6 0.0 copy-start.2
  0.6 0.0 copy-start.3
  0.7 0.8 %reshape.11.cw_ref = f32[8,1024]{1,0:T(8,128)S(1)} reshape(f32[8192]{0:T(1024)} %param.8) | data formatting | bytes 65536 | tf_op jit(solution)/shard_map/reshape | solution.py:387
  1.4 0.0 copy-done.2
  1.4 0.0 copy-done.3
  1.5 0.0 copy-start
  1.5 1.2 %copy-done = bf16[1024,512]{1,0:T(8,128)(2,1)S(1)} copy-done((bf16[1024,512]{1,0:T(8,128)(2,1)S(1)}, bf16[1024,512]{1,0:T(8,128)(2,1)}, u32[]{:S(2)}) %copy-start) | copy-done | bytes 1048600
  2.7 0.0 copy-start.1
  2.7 0.9 %copy-done.1 = bf16[256,512]{1,0:T(8,128)(2,1)S(1)} copy-done((bf16[256,512]{1,0:T(8,128)(2,1)S(1)}, bf16[256,512]{1,0:T(8,128)(2,1)}, u32[]{:S(2)}) %copy-start.1) | copy-done | bytes 262168
  3.6 40.2 %shard_map.68 = (f32[256,512]{1,0:T(8,128)S(1)}, f32[256,512]{1,0:T(8,128)S(1)}) custom-call(bf16[256,512]{1,0:T(8,128)(2,1)S(1)} %copy-done.1, bf16[1024,512]{1,0:T(8,128)(2,1)S(1)} %copy-done, f32[1,256]{1,0:T(1,128)S(1)} %bitcast.1, f32[8,1024]{1,0:T(8,128)S(1)} %reshape.11.cw_ref, s32[2,24]{1,0:T(2,128)S(1)} %copy-done.3), custom_call_target="tpu_custom_call" | custom-call | tf_op jit(solution)/shard_map/pallas_call | solution.py:371
  43.8 0.8 %copy.9 = f32[256,512]{1,0:T(8,128)} copy(f32[256,512]{1,0:T(8,128)S(1)} %get-tuple-element.4) | data formatting | bytes 1048576
  44.6 0.8 %copy.10 = f32[256,512]{1,0:T(8,128)} copy(f32[256,512]{1,0:T(8,128)S(1)} %get-tuple-element.5) | data formatting | bytes 1048576
Async XLA Ops:
  0.6 0.8 %copy-start.2 = (f32[256]{0:T(256)S(1)}, f32[256]{0:T(256)}, u32[]{:S(2)}) copy-start(f32[256]{0:T(256)} %param.7) | copy-start | bytes 3076
  0.6 0.8 %copy-start.3 = (s32[2,24]{1,0:T(2,128)S(1)}, s32[2,24]{1,0:T(2,128)}, u32[]{:S(2)}) copy-start(s32[2,24]{1,0:T(2,128)} %band_ref.1) | copy-start | bytes 580
  1.5 1.2 %copy-start = (bf16[1024,512]{1,0:T(8,128)(2,1)S(1)}, bf16[1024,512]{1,0:T(8,128)(2,1)}, u32[]{:S(2)}) copy-start(bf16[1024,512]{1,0:T(8,128)(2,1)} %c_ref.1) | copy-start | bytes 3145732
  2.7 0.9 %copy-start.1 = (bf16[256,512]{1,0:T(8,128)(2,1)S(1)}, bf16[256,512]{1,0:T(8,128)(2,1)}, u32[]{:S(2)}) copy-start(bf16[256,512]{1,0:T(8,128)(2,1)} %t_ref.1) | copy-start | bytes 786436

commit v2 on v1

--- a/solution.py
+++ b/solution.py
@@ -11,7 +11,7 @@
 SMOOTHING_TEMP = 0.05
 EPSILON = 1e-06
 LANES = 128
-CHUNKS = 4
+CHUNKS = 8
 OWN, NEAR, FAR = 0, 1, 2
 MESH = pl.DeviceIdType.MESH
 F32 = jnp.float32
@@ -36,10 +36,10 @@
 def body(
     wide_size, narrow_size, scale,
     t_ref, c_ref, tw_ref, cw_ref, band_ref, gt_ref, gc_ref,
-    tn, cn, kmat, plan, aux, aux_in, rs, rr, cs, cr,
+    t_in, c_in, cw_in, own_cw, tn, cn, kmat, plan, aux, aux_in, rs, rr, cs, cr,
     far_out, far_in, near_sum, near_out, near_in, own_pull,
     pair_out, pair_in, cross_out, cross_in,
-    bulk_sem, relay_sem, aux_sem, row_sem, col_sem, far_sem, near_sem, pair_sem, cross_sem,
+    bulk_sem, relay_sem, aux_sem, row_sem, col_sem, far_sem, near_sem, pair_sem, cross_sem, load_sem,
 ):
     w = lax.axis_index("wide")
     n = lax.axis_index("narrow")
@@ -63,6 +63,17 @@
             device_id=(wide, narrow), device_id_type=MESH,
         )
 
+    loads = [
+        pltpu.make_async_copy(t_ref, t_in, load_sem.at[0]),
+        pltpu.make_async_copy(cw_ref.at[pl.ds(pl.multiple_of(w * slab, slab), slab)], cw_in, load_sem.at[1]),
+    ]
+    pieces = [pl.ds(i * (slab // narrow_size), slab // narrow_size) for i in range(narrow_size)]
+    loads += [
+        pltpu.make_async_copy(c_ref.at[at], c_in.at[at], load_sem.at[2 + i]) for i, at in enumerate(pieces)
+    ]
+    for item in loads:
+        item.start()
+
     barrier = pltpu.get_barrier_semaphore()
 
     def greet(wide, narrow):
@@ -81,7 +92,6 @@
     def _():
         greet(near2, n)
 
-    tn[OWN] = normalize(t_ref[...])
     for side in range(3):
         for block in range(blocks):
             k = side * blocks + block
@@ -90,6 +100,9 @@
             )
         aux[side, 2:3, 0:rows] = tw_ref[...]
 
+    loads[0].wait()
+    tn[OWN] = normalize(t_in[...])
+
     @pl.when(jnp.logical_not(has_far))
     def _():
         tn[FAR] = jnp.zeros((rows, features), BF16)
@@ -128,45 +141,52 @@
     for item in bulk:
         item.start()
 
-    for quarter in range(narrow_size):
-        at = pl.ds(quarter * (slab // narrow_size), slab // narrow_size)
-        cn[at, :] = normalize(c_ref[at, :])
-
-    def kernel_block(shard, mask_ref):
-        sums = []
-        for block in range(rows // block_rows):
-            at = slice(block * block_rows, (block + 1) * block_rows)
-            inner = lax.dot_general(
-                tn[shard, at, :], cn[...], (((1,), (1,)), ((), ())), preferred_element_type=F32
-            )
-            entries = jnp.where(mask_ref[block:block + 1, :] > 0, jnp.exp(inner * scale), 0.0)
-            kmat[shard, at, :] = entries
-            total = entries[:, 0:LANES]
-            for j in range(1, blocks):
-                total = total + entries[:, j * LANES:(j + 1) * LANES]
-            sums.append(total)
-        return jnp.concatenate(sums, axis=0)
+    for i, at in enumerate(pieces):
+        loads[2 + i].wait()
+        cn[at, :] = normalize(c_in[at, :])
+    loads[1].wait()
+    own_cw[...] = cw_in[...].reshape(1, slab)
+
+    def kernel_block(shard, mask_ref, block):
+        at = slice(block * block_rows, (block + 1) * block_rows)
+        inner = lax.dot_general(
+            tn[shard, at, :], cn[...], (((1,), (1,)), ((), ())), preferred_element_type=F32
+        )
+        entries = jnp.where(mask_ref[block:block + 1, :] > 0, jnp.exp(inner * scale), 0.0)
+        kmat[shard, at, :] = entries
+        total = entries[:, 0:LANES]
+        for j in range(1, blocks):
+            total = total + entries[:, j * LANES:(j + 1) * LANES]
+        rs[0, slot_of[shard], :, at] = lane_sums(total)
 
     slot_of = {NEAR: 0, OWN: 1, FAR: 2}
-    rs[0, slot_of[OWN]] = lane_sums(kernel_block(OWN, aux.at[1]))
-
-    for i in range(CHUNKS):
+    per_block = CHUNKS * block_rows // rows
+
+    def pass_on(i):
         bulk[i].wait_recv()
 
         @pl.when(has_near2)
-        def _(i=i):
+        def _():
             relay[i].start()
 
+    blocks_of_rows = rows // block_rows
+    for block in range(blocks_of_rows):
+        pass_on(block)
+        kernel_block(OWN, aux.at[1], block)
+    for i in range(blocks_of_rows, CHUNKS):
+        pass_on(i)
     aux_near.wait_recv()
-    rs[0, slot_of[NEAR]] = lane_sums(kernel_block(NEAR, aux_in.at[0]))
-
-    @pl.when(has_far)
-    def _():
-        aux_far.wait_recv()
-        for i in range(CHUNKS):
-            relay[i].wait_recv()
-
-    rs[0, slot_of[FAR]] = lane_sums(kernel_block(FAR, aux_in.at[1]))
+    for block in range(blocks_of_rows):
+        kernel_block(NEAR, aux_in.at[0], block)
+    for block in range(blocks_of_rows):
+        @pl.when(has_far)
+        def _(block=block):
+            if block == 0:
+                aux_far.wait_recv()
+            for i in range(block * per_block, (block + 1) * per_block):
+                relay[i].wait_recv()
+
+        kernel_block(FAR, aux_in.at[1], block)
 
     weights = {
         OWN: tw_ref[...],
@@ -174,7 +194,7 @@
         FAR: aux_in[1, 2:3, 0:rows],
     }
     cols = [slice(j * LANES, (j + 1) * LANES) for j in range(blocks)]
-    own_mass = cw_ref[pl.ds(w, 1), :]
+    own_mass = own_cw[...]
     col_scale = None
     row_scale = None
     for sweep in range(SWEEPS):
@@ -272,32 +292,38 @@
             )
         return total
 
+    near_send = [
+        copy(near_out.at[part[i]], near_in.at[part[i]], near_sem, (i,), near, n) for i in range(CHUNKS)
+    ]
+
+    def pass_near(first, last):
+        for i in range(first, last):
+            @pl.when(has_near2)
+            def _(i=i):
+                far_send[i].wait_recv()
+
+            near_out[part[i], :] = (near_sum[part[i], :] + far_in[part[i], :].astype(F32)).astype(BF16)
+            near_send[i].start()
+
     pair_send = [copy(pair_out.at[i], pair_in.at[i], pair_sem, (i,), w, pair) for i in range(2)]
     pair_out[0] = push(cross_pair).astype(BF16)
     pair_send[0].start()
     near_sum[...] = pull(NEAR, near_mass)
+    pass_near(0, 2)
     own_push = push(cross)
     pair_send[0].wait_recv()
     cross_out[...] = (own_push + pair_in[0].astype(F32)).astype(BF16)
     cross_send = copy(cross_out, cross_in, cross_sem, (0,), w, cross)
     cross_send.start()
+    pass_near(2, 5)
     pair_out[1] = push(pair).astype(BF16)
     pair_send[1].start()
 
-    near_send = [
-        copy(near_out.at[part[i]], near_in.at[part[i]], near_sem, (i,), near, n) for i in range(CHUNKS)
-    ]
-    for i in range(CHUNKS):
-        @pl.when(has_near2)
-        def _(i=i):
-            far_send[i].wait_recv()
-
-        near_out[part[i], :] = (near_sum[part[i], :] + far_in[part[i], :].astype(F32)).astype(BF16)
-        near_send[i].start()
+    pass_near(5, CHUNKS)
 
     own_pull[...] = pull(OWN, own_mass_rows)
     at = pl.ds(pl.multiple_of(n * quarter_rows, quarter_rows), quarter_rows)
-    mass = to_columns(cw_ref[pl.ds(w, 1), at])
+    mass = to_columns(own_cw[:, at])
     own_rows = cn[at, :].astype(F32)
     own_push = push(n)
     pair_send[1].wait_recv()
@@ -342,10 +368,15 @@
     rows, features = treated.shape
     slab = control.shape[0]
     quarter = slab // narrow_size
+    hbm = pl.BlockSpec(memory_space=pl.ANY)
     vmem = pl.BlockSpec(memory_space=pltpu.VMEM)
     dma = lambda *shape: pltpu.SemaphoreType.DMA((2,) + shape)
     block = pltpu.VMEM((rows, features), BF16)
     scratch = [
+        pltpu.VMEM((rows, features), BF16),
+        pltpu.VMEM((slab, features), BF16),
+        pltpu.VMEM((slab,), F32),
+        pltpu.VMEM((1, slab), F32),
         pltpu.VMEM((3, rows, features), BF16),
         pltpu.VMEM((slab, features), BF16),
         pltpu.VMEM((3, rows, slab), F32),
@@ -366,27 +397,37 @@
         pltpu.VMEM((quarter, features), BF16),
         dma(CHUNKS), dma(CHUNKS), dma(2), dma(SWEEPS, 4), dma(SWEEPS, narrow_size - 1),
         dma(CHUNKS), dma(CHUNKS), dma(2), dma(1),
+        pltpu.SemaphoreType.DMA((2 + narrow_size,)),
     ]
     scale = 1.0 / (features * SMOOTHING_TEMP)
-    return pl.pallas_call(
+    outputs = pl.pallas_call(
         functools.partial(body, wide_size, narrow_size, scale),
         out_shape=(
             jax.ShapeDtypeStruct((rows, features), F32),
             jax.ShapeDtypeStruct((quarter, features), F32),
         ),
-        in_specs=[vmem] * 5,
+        in_specs=[hbm, hbm, vmem, hbm, vmem],
         out_specs=(vmem, vmem),
         scratch_shapes=scratch,
         compiler_params=pltpu.CompilerParams(
-            collective_id=0, has_side_effects=True, vmem_limit_bytes=40 * 1024 * 1024
+            collective_id=0, has_side_effects=True, vmem_limit_bytes=60 * 1024 * 1024
         ),
     )(
         treated,
         control,
         treated_weight.reshape(1, rows),
-        control_weight.reshape(wide_size, slab),
+        control_weight,
         band,
     )
+    def store_body(a, b, c, d):
+        c[...] = a[...]
+        d[...] = b[...]
+    return pl.pallas_call(
+        store_body,
+        out_shape=tuple(jax.ShapeDtypeStruct(out.shape, out.dtype) for out in outputs),
+        in_specs=[vmem] * 2,
+        out_specs=(vmem, vmem),
+    )(*outputs)
 
 
 def solution(mesh):

time: 45.7 us -> 44.8 us (0.980)
  local copies, waits for them, and re-layouts: 4.55 us -> 0 us
  Pallas kernels: 40.2 us -> 44 us
    unnamed x10 -> x0, local copies, waits for them, and re-layouts: 3.77 us -> none
    pallas_call x0 -> x1, Pallas kernels: none -> 2.2 us  [shards(): pl.pallas_call(store_body, out_shape=tuple((jax.ShapeDtypeStruct(out.shap...]
    pallas_call x1, Pallas kernels: 40.2 us -> 41.8 us  [shards(): pl.pallas_call(functools.partial(body, wide_size, narrow_size, scale), ou...]
    reshape x1 -> x0, local copies, waits for them, and re-layouts: 0.78 us -> none  [shards(): control_weight.reshape(wide_size, slab)]
where the time goes in v2:
time: 44.8 us; the launch traced here: 44.6 us
  Pallas kernels  44 us (98%)
  between operations  0.64 us (1%)
    pallas_call x1, Pallas kernels, shards(): pl.pallas_call(functools.partial(body, wide_size, narrow_size, scale), ou...  41.8 us
    pallas_call x1, Pallas kernels, shards(): pl.pallas_call(store_body, out_shape=tuple((jax.ShapeDtypeStruct(out.shap...  2.2 us

profile of v2, /device:TPU:0, one launch (start us, length us, event | category | flops | bytes accessed | tf_op | source)
XLA Modules:
  0.0 44.6 jit_solution(16187166033890345591)
XLA Ops:
  0.6 41.8 %shard_map.68 = (f32[256,512]{1,0:T(8,128)}, f32[256,512]{1,0:T(8,128)}) custom-call(bf16[256,512]{1,0:T(8,128)(2,1)} %t_ref.1, bf16[1024,512]{1,0:T(8,128)(2,1)} %c_ref.1, f32[1,256]{1,0:T(1,128)} %bitcast.1, f32[8192]{0:T(1024)} %cw_ref.1, s32[2,24]{1,0:T(2,128)} %band_ref.1), custom_call_target="tpu_custom_call" | custom-call | tf_op jit(solution)/shard_map/pallas_call | solution.py:403
  42.4 2.2 %shard_map.69 = (f32[256,512]{1,0:T(8,128)}, f32[256,512]{1,0:T(8,128)}) custom-call(f32[256,512]{1,0:T(8,128)} %get-tuple-element.4.a, f32[256,512]{1,0:T(8,128)} %get-tuple-element.5.b), custom_call_target="tpu_custom_call" | custom-call | tf_op jit(solution)/shard_map/pallas_call | solution.py:425
